TPU v7x, 128 devices: a whole 4x4x4 slice. The times are simulated.
128 devices in a mesh: shot: 8 (over z_lo, y), rcv: 16 (over x, z_hi, core).
Axes of the slice: x: 4, y: 4, z: 4 (z_hi: 2, z_lo: 2; z = z_hi * 2 + z_lo), core: 2. Of those that a mesh axis runs over, the one named last changes fastest.
Arguments:
- traces: bfloat16 [512, 1024, 2048], P('shot', 'rcv'), may hold values from -6 to 6
- phases: int32 [512, 64], P('shot'), may hold values from 0 to 63
- bins: int32 [256], replicated, may hold values from 1 to 1023
- observed: float32 [64, 2, 1024, 256], P('shot', None, 'rcv'), may hold values from -6 to 6
Outputs:
- residual_traces: float32 [64, 1024, 2048], P('shot', None, 'rcv')
All inputs are finite; a program needn't handle non-finite values.
Results may differ from a plain program's by a relative error of at most 0.0015.
Values sent between devices are 32-bit elements; how exact they have to be, the bound alone decides.
A program may use at most 128 MiB of HBM per device.

v0:
```python
import math

import jax
import jax.numpy as jnp
from jax import lax
from jax.sharding import PartitionSpec as P


def angle_tables(bins, time_index, samples):
    phase_grid = time_index[:, None] * bins[None, :] % samples
    angle_grid = phase_grid.astype(jnp.float32) * (2.0 * math.pi / samples)
    return (jnp.cos(angle_grid), jnp.sin(angle_grid))


def body(traces, phases, bins, observed):
    shots_local, rcv_local, samples = traces.shape
    freqs = bins.shape[0]
    supers = phases.shape[1]
    n_shot = lax.axis_size("shot")
    n_rcv = lax.axis_size("rcv")
    high = lax.Precision.HIGHEST
    cos_table, sin_table = angle_tables(bins, jnp.arange(samples, dtype=jnp.int32), samples)
    forward_table = jnp.concatenate([cos_table, -sin_table], axis=1).astype(jnp.bfloat16)
    spectrum = jnp.dot(
        traces.reshape(shots_local * rcv_local, samples),
        forward_table,
        preferred_element_type=jnp.float32,
    )
    spectrum = (spectrum * (1.0 / math.sqrt(samples))).reshape(shots_local, rcv_local, 2, freqs)
    spec_real = spectrum[:, :, 0, :]
    spec_imag = spectrum[:, :, 1, :]
    code_angle = phases.astype(jnp.float32) * (2.0 * math.pi / 64.0)
    shots_all = shots_local * n_shot
    code_cos = jnp.cos(code_angle) / math.sqrt(shots_all)
    code_sin = jnp.sin(code_angle) / math.sqrt(shots_all)
    super_local = supers // n_shot
    real_part = jnp.einsum("se,srf->erf", code_cos, spec_real, precision=high) - jnp.einsum(
        "se,srf->erf", code_sin, spec_imag, precision=high
    )
    imag_part = jnp.einsum("se,srf->erf", code_sin, spec_real, precision=high) + jnp.einsum(
        "se,srf->erf", code_cos, spec_imag, precision=high
    )
    whole_sum = lax.psum(jnp.stack([real_part, imag_part], axis=1), "shot")
    encoded = lax.dynamic_slice_in_dim(
        whole_sum, lax.axis_index("shot") * super_local, super_local, 0
    )
    residual = encoded - observed
    block_width = samples // n_rcv
    inv_scale = 1.0 / math.sqrt(2 * freqs)
    time_index = lax.axis_index("rcv") * block_width + jnp.arange(block_width, dtype=jnp.int32)
    cos_block, sin_block = angle_tables(bins, time_index, samples)
    inverse = jnp.stack([cos_block.T, -sin_block.T], axis=0) * inv_scale
    return jnp.einsum(
        "ecrf,cft->ert",
        lax.all_gather(residual, "rcv", axis=2, tiled=True),
        inverse,
        precision=high,
    )


def solution(mesh):
    in_specs = (P("shot", "rcv", None), P("shot", None), P(), P("shot", None, "rcv", None))
    out_specs = P("shot", None, "rcv")
    return jax.shard_map(body, mesh=mesh, in_specs=in_specs, out_specs=out_specs, check_vma=False)
```

profile of v0, /device:TPU:1, one launch (start us, length us, event | category | flops | bytes accessed | tf_op | source)
XLA Modules:
  0.0 428.5 jit_solution(8950309935913667186)
XLA Ops:
  6.5 0.0 all-reduce.2.cloned.1.call-start
  6.5 9.4 %cosine_convert_fusion = (bf16[2048,256]{1,0:T(8,128)(2,1)S(1)}, bf16[2048,256]{1,0:T(8,128)(2,1)S(1)}) fusion(s32[256]{0:T(256)} %param.6), kind=kLoop, calls=%fused_computation.23 | loop fusion | flops 8912896 | bytes 2098176 | tf_op jit(solution)/shard_map/convert
  15.9 14.7 %multiply_bitcast_fusion = f32[4096,512]{0,1:T(8,128)} fusion(bf16[4096,2048]{1,0:T(8,128)(2,1)} %bitcast.45, bf16[2048,256]{1,0:T(8,128)(2,1)S(1)} %get-tuple-element.10, bf16[2048,256]{1,0:T(8,128)(2,1)S(1)} %get-tuple-element.9), kind=kOutput, calls=%fused_computation.1 | convolution fusion | flops 8596226048 | bytes 27262976 | tf_op jit(solution)/shard_map/dot_general | solution.py:24
  30.6 14.2 %reshape.144 = f32[64,64,2,256]{1,0,3,2:T(8,128)} reshape(f32[4096,512]{0,1:T(8,128)} %multiply_bitcast_fusion) | data formatting | bytes 16777216 | tf_op jit(solution)/shard_map/reshape | solution.py:29
  44.8 10.8 %fusion.54 = (f32[64,64,1,256]{1,0,3,2:T(8,128)}, f32[64,64,1,256]{1,0,3,2:T(8,128)}) fusion(f32[64,64,2,256]{1,0,3,2:T(8,128)} %reshape.144), kind=kLoop, calls=%fused_computation.71 | loop fusion | bytes 16777216 | tf_op jit(solution)/shard_map/slice | solution.py:30
  55.6 0.0 copy-start.4
  55.6 8.6 %copy.36 = f32[64,64,1,256]{3,0,1,2:T(8,128)} copy(f32[64,64,1,256]{1,0,3,2:T(8,128)} %get-tuple-element.6) | data formatting | bytes 8388608
  64.2 0.0 copy-done.4
  64.2 0.0 copy-start.1
  64.2 8.1 %fusion.2 = f32[64,64,256]{2,0,1:T(8,128)} fusion(f32[64,64,1,256]{3,0,1,2:T(8,128)} %copy.36, s32[64,64]{1,0:T(8,128)S(1)} %copy-done.4), kind=kOutput, calls=%fused_computation.4 | convolution fusion | flops 805318656 | bytes 8404992 | tf_op jit(solution)/shard_map/se,srf->erf/dot_general | solution.py:37
  72.3 0.0 copy-done.1
  72.3 5.4 %fusion = f32[64,64,256]{2,0,1:T(8,128)} fusion(f32[64,64,1,256]{3,0,1,2:T(8,128)S(1)} %copy-done.1, s32[64,64]{1,0:T(8,128)S(1)} %copy-done.4), kind=kOutput, calls=%fused_computation.2 | convolution fusion | flops 805318656 | bytes 8404992 | tf_op jit(solution)/shard_map/se,srf->erf/dot_general | solution.py:40
  77.7 8.7 %copy.35 = f32[64,64,1,256]{3,0,1,2:T(8,128)} copy(f32[64,64,1,256]{1,0,3,2:T(8,128)} %get-tuple-element.5) | data formatting | bytes 8388608
  86.3 0.0 copy-start
  86.3 0.0 copy-start.2
  86.3 7.7 %subtract_bitcast_fusion = f32[64,1,64,256]{3,0,2,1:T(8,128)S(1)} fusion(f32[64,64,256]{2,0,1:T(8,128)} %fusion.2, f32[64,64,1,256]{3,0,1,2:T(8,128)} %copy.35, s32[64,64]{1,0:T(8,128)S(1)} %copy-done.4), kind=kOutput, calls=%fused_computation.12 | convolution fusion | flops 806367232 | bytes 12599296 | tf_op jit(solution)/shard_map/se,srf->erf/dot_general | solution.py:37
  94.0 0.0 copy-done
  94.1 0.0 copy-done.2
  94.1 4.1 add_bitcast_fusion
  98.2 3.8 pad_maximum_fusion
  102.1 0.0 copy-start.3
  102.1 0.0 all-reduce.2.cloned.1.call-update
  102.1 0.0 copy-start.5
  102.1 0.0 all-gather.2.cloned.1.call-start
  102.2 187.7 %all-reduce.2.cloned.1.call-done = f32[64,2,64,256]{3,0,2,1:T(8,128)} async-done(((f32[64,2,64,256]{3,0,2,1:T(8,128)}), f32[64,2,64,256]{3,0,2,1:T(8,128)}) %all-reduce.2.cloned.1.call-update) | async-done | bytes 8388624 | tf_op jit(solution)/shard_map/psum | solution.py:43
  289.9 0.0 copy-done.3
  289.9 2.8 copy_subtract_fusion
  292.7 0.0 all-gather.2.cloned.1.call-update
  292.8 0.0 copy-done.5
  292.8 0.6 fusion.30
  293.4 109.1 %all-gather.2.cloned.1.call-done = f32[8,2,1024,256]{3,0,2,1:T(8,128)} async-done(((f32[8,2,64,256]{3,0,2,1:T(8,128)}), f32[8,2,1024,256]{3,0,2,1:T(8,128)}) %all-gather.2.cloned.1.call-update) | async-done | bytes 16777232 | tf_op jit(solution)/shard_map/all_gather | solution.py:55
  402.4 16.5 %fusion.22 = f32[8,1024,128,1]{2,0,1,3:T(8,128)S(1)} fusion(f32[8,2,1024,256]{3,0,2,1:T(8,128)} %all-gather.2.cloned.1.call-done, f32[1,256,128]{2,1,0:T(8,128)S(1)} %get-tuple-element.8, f32[1,256,128]{2,1,0:T(8,128)S(1)} %get-tuple-element.7), kind=kOutput, calls=%fused_computation.30 | convolution fusion | flops 6442582016 | bytes 21233664 | tf_op jit(solution)/shard_map/ecrf,cft->ert/dot_general | solution.py:53
  418.9 2.8 copy.39
  (1 shorter events, 0.0 us)
Async XLA Ops:
  6.5 283.3 %all-reduce.2.cloned.1.call-start = ((), (), s32[]{:S(2)}) async-start(), calls=%async_computation | async-start | bytes 16777216 | tf_op jit(solution)/shard_map/psum | solution.py:43
  55.6 8.6 %copy-start.4 = (s32[64,64]{1,0:T(8,128)S(1)}, s32[64,64]{1,0:T(8,128)}, u32[]{:S(2)}) copy-start(s32[64,64]{1,0:T(8,128)} %param.5) | copy-start | bytes 49156
  64.2 8.1 %copy-start.1 = (f32[64,64,1,256]{3,0,1,2:T(8,128)S(1)}, f32[64,64,1,256]{3,0,1,2:T(8,128)}, u32[]{:S(2)}) copy-start(f32[64,64,1,256]{3,0,1,2:T(8,128)} %copy.36) | copy-start | bytes 12582916
  86.3 7.7 %copy-start = (f32[64,64,1,256]{3,0,1,2:T(8,128)S(1)}, f32[64,64,1,256]{3,0,1,2:T(8,128)}, u32[]{:S(2)}) copy-start(f32[64,64,1,256]{3,0,1,2:T(8,128)} %copy.35) | copy-start | bytes 12582916
  86.3 7.7 %copy-start.2 = (f32[64,64,256]{2,0,1:T(8,128)S(1)}, f32[64,64,256]{2,0,1:T(8,128)}, u32[]{:S(2)}) copy-start(f32[64,64,256]{2,0,1:T(8,128)} %fusion) | copy-start | bytes 12582916
  102.1 187.8 %copy-start.3 = (f32[8,2,64,256]{3,2,1,0:T(8,128)S(1)}, f32[8,2,64,256]{3,2,1,0:T(8,128)}, u32[]{:S(2)}) copy-start(f32[8,2,64,256]{3,2,1,0:T(8,128)} %param.7) | copy-start | bytes 3145732
  102.1 190.7 %copy-start.5 = (s32[256]{0:T(256)S(1)}, s32[256]{0:T(256)}, u32[]{:S(2)}) copy-start(s32[256]{0:T(256)} %param.6) | copy-start | bytes 3076
  102.1 300.3 %all-gather.2.cloned.1.call-start = ((), (), s32[]{:S(2)}) async-start(), calls=%async_computation.1 | async-start | bytes 17825792 | tf_op jit(solution)/shard_map/all_gather | solution.py:55
Sparse Core Ops, SparseCore 0:
  102.2 187.6 all-reduce.1
  292.9 109.5 all-gather.1
where the time goes:
time: 429 us
  waiting for transfers between devices  297 us (69%)
  matrix products  56.5 us (13%)
  local copies, waits for them, and re-layouts  45 us (10%)
  other arithmetic  16.6 us (4%)
  between operations  13.5 us (3%)
    psum x1, waiting for transfers between devices, body(): whole_sum = lax.psum(jnp.stack([real_part, imag_part], axis=1), 'shot')  188 us
    all_gather x1, waiting for transfers between devices, body(): lax.all_gather(residual, 'rcv', axis=2, tiled=True)  109 us
    unnamed x14, local copies, waits for them, and re-layouts  17.3 us
    dot_general x1, matrix products, body(): jnp.einsum('ecrf,cft->ert', lax.all_gather(residual, 'rcv', axis=2, tiled...  16.5 us
    dot_general x1, matrix products, body(): jnp.dot(traces.reshape(shots_local * rcv_local, samples), forward_table,...  14.7 us
    reshape x1, local copies, waits for them, and re-layouts, body(): (spectrum * (1.0 / math.sqrt(samples))).reshape(shots_local, rcv_local, 2...  14.2 us
    slice x1, local copies, waits for them, and re-layouts, body(): spec_real = spectrum[:, :, 0, :]  10.8 us
    another operation x1, other arithmetic  9.36 us
  transfers between devices with their start and end apart: 2, of which 2 were waited for; matrix products, arithmetic and copies ran while one was open for 0% of the time, Pallas kernels for 0%

commit v1 on v0

v1 whole, which is shorter than its diff:
```python
import functools
import math

import jax
import jax.numpy as jnp
from jax import lax
from jax.experimental import pallas as pl
from jax.experimental.pallas import tpu as pltpu
from jax.sharding import PartitionSpec as P

MESH = pl.DeviceIdType.MESH
F32 = jnp.float32
BF16 = jnp.bfloat16

NT = 2048
NF = 256
SL = 64
RL = 64
NE = 64
G = 16
CH = 8
NCH = RL // CH
ET = 8
NX = 4
NY = 4


def trig(k):
    q = lax.shift_right_logical(k + 256, 9)
    x = (k - q * 512).astype(F32) * (2.0 * math.pi / NT)
    q = q & 3
    x2 = x * x
    s = x + x * x2 * (-1.0 / 6 + x2 * (1.0 / 120 + x2 * (-1.0 / 5040 + x2 * (1.0 / 362880))))
    c = 1.0 + x2 * (-0.5 + x2 * (1.0 / 24 + x2 * (-1.0 / 720 + x2 * (1.0 / 40320 - x2 * (1.0 / 3628800)))))
    odd = (q & 1) == 1
    cos = jnp.where(odd, s, c)
    sin = jnp.where(odd, c, s)
    cos = jnp.where((q == 1) | (q == 2), -cos, cos)
    sin = jnp.where(q >= 2, -sin, sin)
    return cos, sin


def split(v):
    hi = v.astype(BF16)
    lo = (v - hi.astype(F32)).astype(BF16)
    return hi, lo


def kernel(
    traces, phases, bins, observed, out,
    tr, ft, code, spec, part, y1a, y1b, y2l, y2r, zrv, res, zhrv, thi, tlo, obuf, base, obs,
    tr_sem, obs_sem, own_sem, y1s, y1r, y2s, y2rs, zs, zr, zhs, zhr, xs, xr,
):
    shot = lax.axis_index("shot")
    rcv = lax.axis_index("rcv")
    y = shot % 4
    zl = shot // 4
    x = rcv // 4
    zh = (rcv // 2) % 2
    core = rcv % 2

    def at_y(d):
        return {"shot": zl * 4 + (y + d + 4) % 4, "rcv": rcv}

    left, right = at_y(-1), at_y(1)
    pair = {"shot": (1 - zl) * 4 + y, "rcv": rcv}
    far = {"shot": shot, "rcv": x * 4 + (1 - zh) * 2 + core}

    def owner(dx, dc):
        xx, cc = (x + dx) % 4, (core + dc) % 2
        return xx, cc, {"shot": shot, "rcv": xx * 4 + zh * 2 + cc}

    others = [(dx, dc) for dx in (2, 1, 3, 0) for dc in (0, 1) if (dx, dc) != (0, 0)]

    barrier = pltpu.get_barrier_semaphore()
    partners = [left, right, pair, far] + [owner(dx, dc)[2] for dx, dc in others]
    for d in partners:
        pl.semaphore_signal(barrier, inc=1, device_id=d, device_id_type=MESH)

    def load(g):
        return pltpu.make_async_copy(traces.at[:, pl.ds(g * G, G), :], tr.at[g], tr_sem.at[g])

    def load_observed(h):
        return pltpu.make_async_copy(
            observed.at[:, pl.ds(h * 128, 128)], obs.at[h], obs_sem.at[h]
        )

    for g in range(RL // G):
        load(g).start()
    for h in range(2):
        load_observed(h).start()

    cc, cs = trig(phases[...] * 32)
    cc, cs = cc * (1.0 / 1024), cs * (1.0 / 1024)
    mat = jnp.concatenate(
        [jnp.concatenate([cc, cs], axis=1), jnp.concatenate([-cs, cc], axis=1)], axis=0
    ).T
    rows = []
    for yy in range(NY):
        for zz in range(2):
            for c in range(2):
                at = c * NE + zz * 32 + yy * 8
                rows.append(mat[at : at + 8, :])
    mat = jnp.concatenate(rows, axis=0)
    chi, clo = split(mat)
    code[...] = jnp.concatenate(
        [jnp.concatenate([chi, chi], axis=1), jnp.concatenate([clo, clo], axis=1)], axis=0
    )

    row = lax.broadcasted_iota(jnp.int32, (128, NF), 0)
    b = jnp.broadcast_to(bins[...], (128, NF))
    cosb, sinb = trig((row * b) & (NT - 1))
    base[0] = cosb
    base[1] = sinb
    row16 = lax.broadcasted_iota(jnp.int32, (16, NF), 0)
    cosa, sina = trig((row16 * 128 * b[:16]) & (NT - 1))
    base[2, 0:16] = cosa
    base[3, 0:16] = sina

    def forward_rows(a, _):
        ca, sa = base[2, pl.ds(a, 1), :], base[3, pl.ds(a, 1), :]
        cb, sb = base[0], base[1]
        at = pl.ds(pl.multiple_of(a * 128, 128), 128)
        ft[at, 0:NF] = (ca * cb - sa * sb).astype(BF16)
        ft[at, NF : 2 * NF] = (-(sa * cb + ca * sb)).astype(BF16)
        return 0

    lax.fori_loop(0, 16, forward_rows, 0)

    def inverse_table():
        scale = 1.0 / math.sqrt(2 * NF)
        blk = lax.broadcasted_iota(jnp.int32, (128, NF), 0)
        blk = ((blk // 2) * 4 + zh * 2 + blk % 2) & 15
        ca, sa = trig((blk * 128 * b) & (NT - 1))
        ca, sa = (ca * scale).T, (sa * scale).T
        cb, sb = base[0].T, base[1].T
        for i in range(2 * NX):
            ci, si = ca[:, i : i + 1], sa[:, i : i + 1]
            cols = slice(i * 128, (i + 1) * 128)
            hi, lo = split(ci * cb - si * sb)
            thi[0:NF, cols] = hi
            tlo[0:NF, cols] = lo
            hi, lo = split(-(si * cb + ci * sb))
            thi[NF : 2 * NF, cols] = hi
            tlo[NF : 2 * NF, cols] = lo

    def remote(src, dst, send, recv, device):
        return pltpu.make_async_remote_copy(
            src_ref=src, dst_ref=dst, send_sem=send, recv_sem=recv, device_id=device, device_id_type=MESH
        )

    opp, nxt, prv = (y + 2) % 4, (y + 1) % 4, (y + 3) % 4

    def copy(name, i):
        r = pl.ds(i * CH, CH)
        table = {
            "a1": (part.at[opp, 0, :, r], y1a.at[:, r], y1s.at[0, i], y1r.at[0, i], right),
            "b1": (part.at[opp, 1, :, r], y1b.at[:, r], y1s.at[1, i], y1r.at[1, i], left),
            "l1": (part.at[nxt, 1, :, r], y2l.at[1, :, r], y2s.at[0, i], y2rs.at[0, i], right),
            "r0": (part.at[prv, 0, :, r], y2r.at[0, :, r], y2s.at[1, i], y2rs.at[1, i], left),
            "l0": (part.at[nxt, 0, :, r], y2l.at[0, :, r], y2s.at[2, i], y2rs.at[2, i], right),
            "r1": (part.at[prv, 1, :, r], y2r.at[1, :, r], y2s.at[3, i], y2rs.at[3, i], left),
            "z": (part.at[y, 1 - zl, :, r], zrv.at[:, r], zs.at[i], zr.at[i], pair),
            "h": (res.at[:, r], zhrv.at[:, r], zhs.at[i], zhr.at[i], far),
        }
        return remote(*table[name])

    def forward(g):
        load(g).wait()

        def tile(m, _):
            xs_ = tr[g, pl.ds(m * 16, 16)].reshape(16 * G, NT)
            v = jnp.dot(xs_, ft[...], preferred_element_type=F32)
            for q in range(4):
                spec[q, pl.ds(pl.multiple_of(m * 16 * G, 16 * G), 16 * G), :] = v[
                    :, q * 128 : (q + 1) * 128
                ]
            return 0

        lax.fori_loop(0, SL // 16, tile, 0)

    def encode(i):
        for j in range(CH):
            at = pl.ds((i % 2) * CH + j, SL, stride=G)
            re = jnp.concatenate([spec[0, at, :], spec[1, at, :]], axis=1)
            im = jnp.concatenate([spec[2, at, :], spec[3, at, :]], axis=1)
            hi, lo = split(jnp.concatenate([re, im], axis=0))
            both = jnp.dot(
                code[...], jnp.concatenate([hi, lo], axis=0), preferred_element_type=F32
            )
            part[:, :, :, i * CH + j] = (both[0:128] + both[128:256]).reshape(NY, 2, 2, ET, NF)

    def inverse(src, i, which):
        r = pl.ds(i * CH, CH)
        v = jnp.concatenate(
            [src[0, r].reshape(CH * ET, NF), src[1, r].reshape(CH * ET, NF)], axis=1
        )
        hi, lo = split(v)
        hl = jnp.concatenate([hi, lo], axis=0)
        n = CH * ET
        for xx in range(NX):
            cols = slice(xx * 256, (xx + 1) * 256)
            both = jnp.dot(hl, thi[:, cols], preferred_element_type=F32)
            o = both[0:n] + both[n : 2 * n] + jnp.dot(hi, tlo[:, cols], preferred_element_type=F32)
            for c in range(2):
                obuf[xx, c, pl.ds(which * RL + i * CH, CH)] = o[:, c * 128 : (c + 1) * 128].reshape(
                    CH, ET, 128
                )
        from_rcv = x * 4 + core + 2 * (zh if which == 0 else 1 - zh)
        dst = out.at[pl.ds(from_rcv * RL + i * CH, CH)]
        rows_ = pl.ds(which * RL + i * CH, CH)
        for dx, dc in others:
            xx, c, device = owner(dx, dc)
            remote(
                obuf.at[xx, c, rows_], dst, xs.at[xx * 2 + c], xr.at[x * 2 + core], device
            ).start()
        pltpu.make_async_copy(obuf.at[x, core, rows_], dst, own_sem).start()

    def step(i, _):
        @pl.when(i < NCH)
        def _():
            @pl.when(i % 2 == 0)
            def _():
                forward(i // 2)

            encode(i)

        @pl.when(i == 0)
        def _():
            pl.semaphore_wait(barrier, len(partners))

        @pl.when(i < NCH)
        def _():
            for k in ("a1", "b1", "l1", "r0"):
                copy(k, i).start()

        @pl.when(i == 0)
        def _():
            inverse_table()
            for h in range(2):
                load_observed(h).wait()

        @pl.when((i >= 1) & (i < NCH + 1))
        def _():
            k = i - 1
            r = pl.ds(k * CH, CH)
            copy("a1", k).wait_recv()
            part[nxt, 0, :, r] = part[nxt, 0, :, r] + y1a[:, r]
            copy("l0", k).start()
            copy("b1", k).wait_recv()
            part[prv, 1, :, r] = part[prv, 1, :, r] + y1b[:, r]
            copy("r1", k).start()

        @pl.when((i >= 2) & (i < NCH + 2))
        def _():
            k = i - 2
            r = pl.ds(k * CH, CH)
            for name in ("l1", "r0", "l0", "r1"):
                copy(name, k).wait_recv()
            part[y, 1 - zl, :, r] = part[y, 1 - zl, :, r] + y2l[1 - zl, :, r] + y2r[1 - zl, :, r]
            copy("z", k).start()
            res[:, r] = part[y, zl, :, r] + y2l[zl, :, r] + y2r[zl, :, r]
            for p in range(2):
                for j in range(CH):
                    at = k * CH + j
                    rows = pl.ds(p * RL + at, ET, stride=2 * RL)
                    seen = jnp.concatenate([obs[0, rows, :], obs[1, rows, :]], axis=1)
                    res[p, at] = res[p, at] - seen

        @pl.when((i >= 3) & (i < NCH + 3))
        def _():
            k = i - 3
            r = pl.ds(k * CH, CH)
            copy("z", k).wait_recv()
            res[:, r] = res[:, r] + zrv[:, r]
            copy("h", k).start()
            inverse(res, k, 0)

        @pl.when(i >= 4)
        def _():
            k = i - 4
            copy("h", k).wait_recv()
            inverse(zhrv, k, 1)

        return 0

    lax.fori_loop(0, NCH + 4, step, 0)

    def drain(i, _):
        for name in ("a1", "b1", "l1", "r0", "l0", "r1", "z", "h"):
            copy(name, i).wait_send()
        return 0

    lax.fori_loop(0, NCH, drain, 0)
    whole = out.at[pl.ds(0, 2 * RL)]
    pltpu.make_async_copy(obuf.at[x, core], whole, own_sem).wait()
    for dx, dc in others:
        xx, c, device = owner(dx, dc)
        both = remote(obuf.at[xx, c], whole, xs.at[xx * 2 + c], xr.at[xx * 2 + c], device)
        both.wait_send()
        both.wait_recv()


def body(traces, phases, bins, observed):
    dma = pltpu.SemaphoreType.DMA
    vmem = lambda *s: pltpu.VMEM(s, F32)
    whole = pl.BlockSpec(memory_space=pltpu.VMEM)
    anywhere = pl.BlockSpec(memory_space=pl.ANY)
    flops = 2 * (SL * RL * NT * 2 * NF + 4 * 128 * 128 * RL * NF + 3 * 1024 * 512 * 1024)
    rows = pl.pallas_call(
        kernel,
        out_shape=jax.ShapeDtypeStruct((16 * RL, ET, 128), F32),
        in_specs=[anywhere, whole, whole, anywhere],
        out_specs=anywhere,
        scratch_shapes=[
            pltpu.VMEM((RL // G, SL, G, NT), BF16),
            pltpu.VMEM((NT, 2 * NF), BF16),
            pltpu.VMEM((256, 256), BF16),
            vmem(4, SL * G, 128),
            vmem(NY, 2, 2, RL, ET, NF),
            vmem(2, RL, ET, NF),
            vmem(2, RL, ET, NF),
            vmem(2, 2, RL, ET, NF),
            vmem(2, 2, RL, ET, NF),
            vmem(2, RL, ET, NF),
            vmem(2, RL, ET, NF),
            vmem(2, RL, ET, NF),
            pltpu.VMEM((2 * NF, 1024), BF16),
            pltpu.VMEM((2 * NF, 1024), BF16),
            vmem(NX, 2, 2 * RL, ET, 128),
            vmem(4, 128, NF),
            vmem(2, ET * 2 * RL, 128),
            dma((RL // G,)),
            dma((2,)),
            dma,
            dma((2, NCH)),
            dma((2, NCH)),
            dma((4, NCH)),
            dma((4, NCH)),
            dma((NCH,)),
            dma((NCH,)),
            dma((NCH,)),
            dma((NCH,)),
            dma((8,)),
            dma((8,)),
        ],
        compiler_params=pltpu.CompilerParams(
            collective_id=0, has_side_effects=True, vmem_limit_bytes=58 * 2**20
        ),
        cost_estimate=pl.CostEstimate(flops=flops, bytes_accessed=22 * 2**20, transcendentals=0),
    )(traces, phases, bins.reshape(1, NF), observed.reshape(ET * 2 * RL, NF))
    return rows.transpose(1, 0, 2)


def solution(mesh):
    in_specs = (P("shot", "rcv", None), P("shot", None), P(), P("shot", None, "rcv", None))
    out_specs = P("shot", None, "rcv")
    return jax.shard_map(body, mesh=mesh, in_specs=in_specs, out_specs=out_specs, check_vma=False)
```

time: 429 us -> 108 us (0.25)
  waiting for transfers between devices: 297 us -> 0 us
  Pallas kernels: 0 us -> 102 us
  matrix products: 56.5 us -> 0 us
  local copies, waits for them, and re-layouts: 45 us -> 5.01 us
  other arithmetic: 16.6 us -> 0 us
  between operations: 13.5 us -> 0.01 us
    psum x1 -> x0, waiting for transfers between devices: 188 us -> none  [body(): whole_sum = lax.psum(jnp.stack([real_part, imag_part], axis=1), 'shot')]
    all_gather x1 -> x0, waiting for transfers between devices: 109 us -> none  [body(): lax.all_gather(residual, 'rcv', axis=2, tiled=True)]
    pallas_call x0 -> x1, Pallas kernels: none -> 102 us  [body(): pl.pallas_call(kernel, out_shape=jax.ShapeDtypeStruct((16 * RL, ET, 128),...]
    dot_general x6 -> x0, matrix products: 56.5 us -> none  [the longest x1 16.5 us: body(): jnp.einsum('ecrf,cft->ert', lax.all_gather(residual, 'rcv', axis=2, tiled...]
    unnamed x14 -> x0, local copies, waits for them, and re-layouts: 17.3 us -> none
    reshape x1 -> x0, local copies, waits for them, and re-layouts: 14.2 us -> none  [body(): (spectrum * (1.0 / math.sqrt(samples))).reshape(shots_local, rcv_local, 2...]
    another operation x2 -> x0, other arithmetic: 13.2 us -> none
    slice x1 -> x0, local copies, waits for them, and re-layouts: 10.8 us -> none  [body(): spec_real = spectrum[:, :, 0, :]]
  transfers between devices with their start and end apart: 2 -> 0, of which waited for: 2 -> 0; matrix products, arithmetic and copies ran while one was open for 0% -> 0% of each run, Pallas kernels for 0% -> 0%
where the time goes in v1:
time: 108 us; the launch traced here: 107 us
  Pallas kernels  102 us (94%)
  local copies, waits for them, and re-layouts  5.01 us (5%)
    pallas_call x1, Pallas kernels, body(): pl.pallas_call(kernel, out_shape=jax.ShapeDtypeStruct((16 * RL, ET, 128),...  102 us
    transpose x1, local copies, waits for them, and re-layouts, body(): return rows.transpose(1, 0, 2)  5.01 us

profile of v1, /device:TPU:1, one launch (start us, length us, event | category | flops | bytes accessed | tf_op | source)
XLA Modules:
  0.0 107.5 jit_solution(7645729531628632567)
XLA Ops:
  0.0 102.5 %shard_map.46 = f32[1024,8,128]{2,1,0:T(8,128)} custom-call(bf16[64,64,2048]{2,1,0:T(8,128)(2,1)} %traces.1, s32[64,64]{1,0:T(8,128)} %phases.1, s32[1,256]{1,0:T(1,128)} %bitcast.5, f32[1024,256]{1,0:T(8,128)} %bitcast.4), custom_call_target="tpu_custom_call" | custom-call | flops 13958643712 | bytes 23068672 | tf_op jit(solution)/shard_map/pallas_call | solution.py:310
  102.5 5.0 %copy.5 = f32[8,1024,128]{2,1,0:T(8,128)} copy(f32[8,1024,128]{2,0,1:T(8,128)} %bitcast.3) | data formatting | bytes 8388608 | tf_op jit(solution)/shard_map/transpose | solution.py:352

commit v2 on v1

--- a/solution.py
+++ b/solution.py
@@ -18,8 +18,15 @@
 RL = 64
 NE = 64
 G = 16
-CH = 8
+CH = 4
 NCH = RL // CH
+ZS = (12, 13, 15)
+SEQ = (0, 1, 2, 3, 4, 5, 6, 7, 12, 13, 8, 9, 10, 11, 14, 15)
+PG = G // CH
+LAST = RL // G - 1
+LAGS = ((2, ()), (4, ()), (6, (13,)), (8, (12, 14)))
+ZG = 1
+ZAT = (1, 3, 8)
 ET = 8
 NX = 4
 NY = 4
@@ -48,8 +55,8 @@
 
 def kernel(
     traces, phases, bins, observed, out,
-    tr, ft, code, spec, part, y1a, y1b, y2l, y2r, zrv, res, zhrv, thi, tlo, obuf, base, obs,
-    tr_sem, obs_sem, own_sem, y1s, y1r, y2s, y2rs, zs, zr, zhs, zhr, xs, xr,
+    tr, ft, code, spec, part, y1a, y1b, y2l, y2r, zrv, zzrv, res, zhrv, thi, tlo, obuf, base, obs,
+    ph, bn, tr_sem, obs_sem, in_sem, own_sem, y1s, y1r, y2s, y2rs, zs, zr, zhs, zhr, xs, xr,
 ):
     shot = lax.axis_index("shot")
     rcv = lax.axis_index("rcv")
@@ -85,12 +92,17 @@
             observed.at[:, pl.ds(h * 128, 128)], obs.at[h], obs_sem.at[h]
         )
 
-    for g in range(RL // G):
+    load_phases = pltpu.make_async_copy(phases, ph, in_sem.at[0])
+    load_bins = pltpu.make_async_copy(bins, bn, in_sem.at[1])
+    load_bins.start()
+    load_phases.start()
+    for g in (0, LAST, *range(1, LAST)):
         load(g).start()
     for h in range(2):
         load_observed(h).start()
 
-    cc, cs = trig(phases[...] * 32)
+    load_phases.wait()
+    cc, cs = trig(ph[...] * 32)
     cc, cs = cc * (1.0 / 1024), cs * (1.0 / 1024)
     mat = jnp.concatenate(
         [jnp.concatenate([cc, cs], axis=1), jnp.concatenate([-cs, cc], axis=1)], axis=0
@@ -108,7 +120,8 @@
     )
 
     row = lax.broadcasted_iota(jnp.int32, (128, NF), 0)
-    b = jnp.broadcast_to(bins[...], (128, NF))
+    load_bins.wait()
+    b = jnp.broadcast_to(bn[...], (128, NF))
     cosb, sinb = trig((row * b) & (NT - 1))
     base[0] = cosb
     base[1] = sinb
@@ -165,6 +178,20 @@
         }
         return remote(*table[name])
 
+    def zcopy(name, i):
+        r = pl.ds(i * CH, CH)
+        rz = pl.ds((i - LAST * PG) * CH, CH)
+        table = {
+            "zz": (part.at[:, 1 - zl, :, r], zzrv.at[:, :, rz], zs.at[i], zr.at[i], pair),
+            "a1": (part.at[opp, zl, 0, r], y1a.at[0, r], y1s.at[0, i], y1r.at[0, i], right),
+            "b1": (part.at[opp, zl, 1, r], y1b.at[0, r], y1s.at[1, i], y1r.at[1, i], left),
+            "l1": (part.at[nxt, zl, 1, r], y2l.at[0, 1, r], y2s.at[0, i], y2rs.at[0, i], right),
+            "r0": (part.at[prv, zl, 0, r], y2r.at[0, 0, r], y2s.at[1, i], y2rs.at[1, i], left),
+            "l0": (part.at[nxt, zl, 0, r], y2l.at[0, 0, r], y2s.at[2, i], y2rs.at[2, i], right),
+            "r1": (part.at[prv, zl, 1, r], y2r.at[0, 1, r], y2s.at[3, i], y2rs.at[3, i], left),
+        }
+        return remote(*table[name])
+
     def forward(g):
         load(g).wait()
 
@@ -181,7 +208,7 @@
 
     def encode(i):
         for j in range(CH):
-            at = pl.ds((i % 2) * CH + j, SL, stride=G)
+            at = pl.ds((i % PG) * CH + j, SL, stride=G)
             re = jnp.concatenate([spec[0, at, :], spec[1, at, :]], axis=1)
             im = jnp.concatenate([spec[2, at, :], spec[3, at, :]], axis=1)
             hi, lo = split(jnp.concatenate([re, im], axis=0))
@@ -216,79 +243,176 @@
             ).start()
         pltpu.make_async_copy(obuf.at[x, core, rows_], dst, own_sem).start()
 
+    def less_observed(k):
+        for p in range(2):
+            for j in range(CH):
+                at = k * CH + j
+                rows = pl.ds(p * RL + at, ET, stride=2 * RL)
+                seen = jnp.concatenate([obs[0, rows, :], obs[1, rows, :]], axis=1)
+                res[p, at] = res[p, at] - seen
+
+    def done(i, lag, earlier):
+        n = i - lag + 1
+        for at in earlier:
+            n = n + jnp.where(i >= at, 1, 0)
+        return jnp.clip(n, 0, NCH)
+
+    def chunk(p):
+        c = p
+        for at in range(1, NCH):
+            jump = SEQ[at] - SEQ[at - 1] - 1
+            if jump:
+                c = c + jnp.where(p >= at, jump, 0)
+        return c
+
+    def early(c):
+        hit = c == ZS[0]
+        for other in ZS[1:]:
+            hit = hit | (c == other)
+        return hit
+
+    def stage0(p):
+        c = chunk(p)
+        z = early(c)
+
+        @pl.when(c < LAST * PG)
+        def _():
+            @pl.when(c % PG == 0)
+            def _():
+                forward(c // PG)
+                encode(c)
+
+            @pl.when(c % PG == 1)
+            def _():
+                lax.fori_loop(c, c + PG - 1, lambda k, _: (encode(k), 0)[1], 0)
+
+        @pl.when(p == 0)
+        def _():
+            pl.semaphore_wait(barrier, len(partners))
+
+        @pl.when(jnp.logical_not(z))
+        def _():
+            for name in ("a1", "b1", "l1", "r0"):
+                copy(name, c).start()
+
+        @pl.when(z)
+        def _():
+            zcopy("zz", c).wait_recv()
+            r = pl.ds(c * CH, CH)
+            part[:, zl, :, r] = part[:, zl, :, r] + zzrv[:, :, pl.ds((c - LAST * PG) * CH, CH)]
+            for name in ("a1", "b1", "l1", "r0"):
+                zcopy(name, c).start()
+
+    def stage1(p, _):
+        c = chunk(p)
+        z = early(c)
+        r = pl.ds(c * CH, CH)
+
+        @pl.when(jnp.logical_not(z))
+        def _():
+            copy("a1", c).wait_recv()
+            part[nxt, 0, :, r] = part[nxt, 0, :, r] + y1a[:, r]
+            copy("l0", c).start()
+            copy("b1", c).wait_recv()
+            part[prv, 1, :, r] = part[prv, 1, :, r] + y1b[:, r]
+            copy("r1", c).start()
+
+        @pl.when(z)
+        def _():
+            zcopy("a1", c).wait_recv()
+            part[nxt, zl, 0, r] = part[nxt, zl, 0, r] + y1a[0, r]
+            zcopy("l0", c).start()
+            zcopy("b1", c).wait_recv()
+            part[prv, zl, 1, r] = part[prv, zl, 1, r] + y1b[0, r]
+            zcopy("r1", c).start()
+
+        return 0
+
+    def stage2(p, _):
+        c = chunk(p)
+        z = early(c)
+        r = pl.ds(c * CH, CH)
+
+        @pl.when(jnp.logical_not(z))
+        def _():
+            for name in ("l1", "r0", "l0", "r1"):
+                copy(name, c).wait_recv()
+            part[y, 1 - zl, :, r] = part[y, 1 - zl, :, r] + y2l[1 - zl, :, r] + y2r[1 - zl, :, r]
+            copy("z", c).start()
+            res[:, r] = part[y, zl, :, r] + y2l[zl, :, r] + y2r[zl, :, r]
+            less_observed(c)
+
+        @pl.when(z)
+        def _():
+            for name in ("l1", "r0", "l0", "r1"):
+                zcopy(name, c).wait_recv()
+            res[:, r] = part[y, zl, :, r] + y2l[0, :, r] + y2r[0, :, r]
+            less_observed(c)
+            copy("h", c).start()
+            inverse(res, c, 0)
+
+        return 0
+
+    def stage3(p, _):
+        c = chunk(p)
+
+        @pl.when(jnp.logical_not(early(c)))
+        def _():
+            r = pl.ds(c * CH, CH)
+            copy("z", c).wait_recv()
+            res[:, r] = res[:, r] + zrv[:, r]
+            copy("h", c).start()
+            inverse(res, c, 0)
+
+        return 0
+
+    def stage4(p, _):
+        c = chunk(p)
+        copy("h", c).wait_recv()
+        inverse(zhrv, c, 1)
+        return 0
+
     def step(i, _):
         @pl.when(i < NCH)
         def _():
-            @pl.when(i % 2 == 0)
-            def _():
-                forward(i // 2)
-
-            encode(i)
-
-        @pl.when(i == 0)
-        def _():
-            pl.semaphore_wait(barrier, len(partners))
-
-        @pl.when(i < NCH)
-        def _():
-            for k in ("a1", "b1", "l1", "r0"):
-                copy(k, i).start()
-
-        @pl.when(i == 0)
+            stage0(i)
+
+        @pl.when(i == 2)
         def _():
             inverse_table()
             for h in range(2):
                 load_observed(h).wait()
 
-        @pl.when((i >= 1) & (i < NCH + 1))
-        def _():
-            k = i - 1
-            r = pl.ds(k * CH, CH)
-            copy("a1", k).wait_recv()
-            part[nxt, 0, :, r] = part[nxt, 0, :, r] + y1a[:, r]
-            copy("l0", k).start()
-            copy("b1", k).wait_recv()
-            part[prv, 1, :, r] = part[prv, 1, :, r] + y1b[:, r]
-            copy("r1", k).start()
-
-        @pl.when((i >= 2) & (i < NCH + 2))
-        def _():
-            k = i - 2
-            r = pl.ds(k * CH, CH)
-            for name in ("l1", "r0", "l0", "r1"):
-                copy(name, k).wait_recv()
-            part[y, 1 - zl, :, r] = part[y, 1 - zl, :, r] + y2l[1 - zl, :, r] + y2r[1 - zl, :, r]
-            copy("z", k).start()
-            res[:, r] = part[y, zl, :, r] + y2l[zl, :, r] + y2r[zl, :, r]
-            for p in range(2):
-                for j in range(CH):
-                    at = k * CH + j
-                    rows = pl.ds(p * RL + at, ET, stride=2 * RL)
-                    seen = jnp.concatenate([obs[0, rows, :], obs[1, rows, :]], axis=1)
-                    res[p, at] = res[p, at] - seen
-
-        @pl.when((i >= 3) & (i < NCH + 3))
-        def _():
-            k = i - 3
-            r = pl.ds(k * CH, CH)
-            copy("z", k).wait_recv()
-            res[:, r] = res[:, r] + zrv[:, r]
-            copy("h", k).start()
-            inverse(res, k, 0)
-
-        @pl.when(i >= 4)
-        def _():
-            k = i - 4
-            copy("h", k).wait_recv()
-            inverse(zhrv, k, 1)
-
-        return 0
-
-    lax.fori_loop(0, NCH + 4, step, 0)
-
-    def drain(i, _):
-        for name in ("a1", "b1", "l1", "r0", "l0", "r1", "z", "h"):
-            copy(name, i).wait_send()
+        @pl.when(i == ZG)
+        def _():
+            forward(LAST)
+            lax.fori_loop(LAST * PG, NCH, lambda k, _: (encode(k), 0)[1], 0)
+
+        for at, c in zip(ZAT, ZS):
+            @pl.when(i == at)
+            def _(c=c):
+                zcopy("zz", c).start()
+
+        for stage, (lag, earlier) in zip((stage1, stage2, stage3, stage4), LAGS):
+            lax.fori_loop(done(i - 1, lag, earlier), done(i, lag, earlier), stage, 0)
+        return 0
+
+    lax.fori_loop(0, NCH + LAGS[3][0] - len(LAGS[3][1]), step, 0)
+
+    def drain(c, _):
+        z = early(c)
+
+        @pl.when(jnp.logical_not(z))
+        def _():
+            for name in ("a1", "b1", "l1", "r0", "l0", "r1", "z"):
+                copy(name, c).wait_send()
+
+        @pl.when(z)
+        def _():
+            for name in ("a1", "b1", "l1", "r0", "l0", "r1", "zz"):
+                zcopy(name, c).wait_send()
+
+        copy("h", c).wait_send()
         return 0
 
     lax.fori_loop(0, NCH, drain, 0)
@@ -304,14 +428,14 @@
 def body(traces, phases, bins, observed):
     dma = pltpu.SemaphoreType.DMA
     vmem = lambda *s: pltpu.VMEM(s, F32)
-    whole = pl.BlockSpec(memory_space=pltpu.VMEM)
-    anywhere = pl.BlockSpec(memory_space=pl.ANY)
+    hbm = pl.BlockSpec(memory_space=pltpu.HBM)
     flops = 2 * (SL * RL * NT * 2 * NF + 4 * 128 * 128 * RL * NF + 3 * 1024 * 512 * 1024)
+    arrays = (traces, phases, bins.reshape(1, NF), observed.reshape(ET * 2 * RL, NF))
     rows = pl.pallas_call(
         kernel,
-        out_shape=jax.ShapeDtypeStruct((16 * RL, ET, 128), F32),
-        in_specs=[anywhere, whole, whole, anywhere],
-        out_specs=anywhere,
+        out_shape=pltpu.VMEM((16 * RL, ET, 128), F32),
+        in_specs=[hbm, hbm, hbm, hbm],
+        out_specs=pl.BlockSpec(memory_space=pl.ANY),
         scratch_shapes=[
             pltpu.VMEM((RL // G, SL, G, NT), BF16),
             pltpu.VMEM((NT, 2 * NF), BF16),
@@ -323,6 +447,7 @@
             vmem(2, 2, RL, ET, NF),
             vmem(2, 2, RL, ET, NF),
             vmem(2, RL, ET, NF),
+            vmem(NY, 2, G, ET, NF),
             vmem(2, RL, ET, NF),
             vmem(2, RL, ET, NF),
             pltpu.VMEM((2 * NF, 1024), BF16),
@@ -330,7 +455,10 @@
             vmem(NX, 2, 2 * RL, ET, 128),
             vmem(4, 128, NF),
             vmem(2, ET * 2 * RL, 128),
+            pltpu.VMEM((SL, NE), jnp.int32),
+            pltpu.VMEM((1, NF), jnp.int32),
             dma((RL // G,)),
+            dma((2,)),
             dma((2,)),
             dma,
             dma((2, NCH)),
@@ -345,10 +473,10 @@
             dma((8,)),
         ],
         compiler_params=pltpu.CompilerParams(
-            collective_id=0, has_side_effects=True, vmem_limit_bytes=58 * 2**20
+            collective_id=0, has_side_effects=True, vmem_limit_bytes=49 * 2**20
         ),
         cost_estimate=pl.CostEstimate(flops=flops, bytes_accessed=22 * 2**20, transcendentals=0),
-    )(traces, phases, bins.reshape(1, NF), observed.reshape(ET * 2 * RL, NF))
+    )(*(pltpu.with_memory_space_constraint(a, pltpu.HBM) for a in arrays))
     return rows.transpose(1, 0, 2)
 
 

time: 108 us -> 99.3 us (0.919)
  Pallas kernels: 102 us -> 96.4 us
  local copies, waits for them, and re-layouts: 5.01 us -> 2.77 us
    pallas_call x1, Pallas kernels: 102 us -> 96.4 us  [body(): pl.pallas_call(kernel, out_shape=pltpu.VMEM((16 * RL, ET, 128), F32), in_...]
    transpose x1, local copies, waits for them, and re-layouts: 5.01 us -> 2.77 us  [body(): return rows.transpose(1, 0, 2)]
where the time goes in v2:
time: 99.3 us; the launch traced here: 99.2 us
  Pallas kernels  96.4 us (97%)
  local copies, waits for them, and re-layouts  2.77 us (3%)
    pallas_call x1, Pallas kernels, body(): pl.pallas_call(kernel, out_shape=pltpu.VMEM((16 * RL, ET, 128), F32), in_...  96.4 us
    transpose x1, local copies, waits for them, and re-layouts, body(): return rows.transpose(1, 0, 2)  2.77 us

profile of v2, /device:TPU:1, one launch (start us, length us, event | category | flops | bytes accessed | tf_op | source)
XLA Modules:
  0.0 99.2 jit_solution(10525328453879356140)
XLA Ops:
  0.0 96.4 %shard_map.46 = f32[1024,8,128]{2,1,0:T(8,128)S(1)} custom-call(bf16[64,64,2048]{2,1,0:T(8,128)(2,1)} %traces.1, s32[64,64]{1,0:T(8,128)} %phases.1, s32[1,256]{1,0:T(1,128)} %bitcast.5, f32[1024,256]{1,0:T(8,128)} %bitcast.4), custom_call_target="tpu_custom_call" | custom-call | flops 13958643712 | bytes 23068672 | tf_op jit(solution)/shard_map/pallas_call | solution.py:434
  96.4 2.8 %copy.5 = f32[8,1024,128]{2,1,0:T(8,128)} copy(f32[8,1024,128]{2,0,1:T(8,128)S(1)} %bitcast.3) | data formatting | bytes 8388608 | tf_op jit(solution)/shard_map/transpose | solution.py:480

commit v3 on v2

--- a/solution.py
+++ b/solution.py
@@ -20,13 +20,18 @@
 G = 16
 CH = 4
 NCH = RL // CH
-ZS = (12, 13, 15)
-SEQ = (0, 1, 2, 3, 4, 5, 6, 7, 12, 13, 8, 9, 10, 11, 14, 15)
+ZS = (12, 13, 14)
+SEQ = (0, 1, 2, 3, 4, 5, 6, 7, 8, 12, 9, 13, 10, 14, 11, 15)
 PG = G // CH
 LAST = RL // G - 1
-LAGS = ((2, ()), (4, ()), (6, (13,)), (8, (12, 14)))
+STEPS = (
+    (1, 4, 4, 4, 4, 6, 7, 8, 9, 11, 12, 13, 14, 18, 18, 21),
+    (3, 4, 5, 6, 6, 8, 10, 11, 12, 13, 15, 17, 20, 21, 22, 23),
+    (5, 5, 8, 8, 9, 11, 11, 13, 13, 16, 17, 17, 21, 22, 24, 25),
+    (6, 7, 8, 10, 10, 12, 12, 13, 15, 16, 20, 20, 23, 23, 24, 26),
+)
 ZG = 1
-ZAT = (1, 3, 8)
+ZAT = (3, 7, 1)
 ET = 8
 NX = 4
 NY = 4
@@ -55,8 +60,8 @@
 
 def kernel(
     traces, phases, bins, observed, out,
-    tr, ft, code, spec, part, y1a, y1b, y2l, y2r, zrv, zzrv, res, zhrv, thi, tlo, obuf, base, obs,
-    ph, bn, tr_sem, obs_sem, in_sem, own_sem, y1s, y1r, y2s, y2rs, zs, zr, zhs, zhr, xs, xr,
+    tr, ft, code, spec, part, y1a, y1b, y2l, y2r, zrv, zzrv, res, zhrv, zgrv, thi, tlo, obuf, base, obs,
+    ph, bn, tr_sem, obs_sem, in_sem, own_sem, y1s, y1r, y2s, y2rs, zs, zr, zhs, zhr, zgs, zgr, xs, xr,
 ):
     shot = lax.axis_index("shot")
     rcv = lax.axis_index("rcv")
@@ -72,6 +77,7 @@
     left, right = at_y(-1), at_y(1)
     pair = {"shot": (1 - zl) * 4 + y, "rcv": rcv}
     far = {"shot": shot, "rcv": x * 4 + (1 - zh) * 2 + core}
+    cross = {"shot": (1 - zl) * 4 + y, "rcv": x * 4 + (1 - zh) * 2 + core}
 
     def owner(dx, dc):
         xx, cc = (x + dx) % 4, (core + dc) % 2
@@ -80,7 +86,7 @@
     others = [(dx, dc) for dx in (2, 1, 3, 0) for dc in (0, 1) if (dx, dc) != (0, 0)]
 
     barrier = pltpu.get_barrier_semaphore()
-    partners = [left, right, pair, far] + [owner(dx, dc)[2] for dx, dc in others]
+    partners = [left, right, pair, far, cross] + [owner(dx, dc)[2] for dx, dc in others]
     for d in partners:
         pl.semaphore_signal(barrier, inc=1, device_id=d, device_id_type=MESH)
 
@@ -96,10 +102,7 @@
     load_bins = pltpu.make_async_copy(bins, bn, in_sem.at[1])
     load_bins.start()
     load_phases.start()
-    for g in (0, LAST, *range(1, LAST)):
-        load(g).start()
-    for h in range(2):
-        load_observed(h).start()
+    load(0).start()
 
     load_phases.wait()
     cc, cs = trig(ph[...] * 32)
@@ -139,6 +142,11 @@
         return 0
 
     lax.fori_loop(0, 16, forward_rows, 0)
+    load(0).wait()
+    for g in (LAST, *range(1, LAST)):
+        load(g).start()
+    for h in range(2):
+        load_observed(h).start()
 
     def inverse_table():
         scale = 1.0 / math.sqrt(2 * NF)
@@ -174,6 +182,7 @@
             "l0": (part.at[nxt, 0, :, r], y2l.at[0, :, r], y2s.at[2, i], y2rs.at[2, i], right),
             "r1": (part.at[prv, 1, :, r], y2r.at[1, :, r], y2s.at[3, i], y2rs.at[3, i], left),
             "z": (part.at[y, 1 - zl, :, r], zrv.at[:, r], zs.at[i], zr.at[i], pair),
+            "g": (part.at[y, 1 - zl, :, r], zgrv.at[:, r], zgs.at[i], zgr.at[i], cross),
             "h": (res.at[:, r], zhrv.at[:, r], zhs.at[i], zhr.at[i], far),
         }
         return remote(*table[name])
@@ -192,6 +201,18 @@
         }
         return remote(*table[name])
 
+    def forward_half(h):
+        def tile(m, _):
+            xs_ = tr[0, pl.ds(m * 32, 32), 8 * h : 8 * h + 8].reshape(32 * 8, NT)
+            v = jnp.dot(xs_, ft[...], preferred_element_type=F32)
+            for q in range(4):
+                for n in range(32):
+                    at = pl.ds(pl.multiple_of((m * 32 + n) * G + 8 * h, 8), 8)
+                    spec[q, at, :] = v[n * 8 : n * 8 + 8, q * 128 : (q + 1) * 128]
+            return 0
+
+        lax.fori_loop(0, SL // 32, tile, 0)
+
     def forward(g):
         load(g).wait()
 
@@ -217,11 +238,10 @@
             )
             part[:, :, :, i * CH + j] = (both[0:128] + both[128:256]).reshape(NY, 2, 2, ET, NF)
 
-    def inverse(src, i, which):
+    def inverse(one, two, i, which):
         r = pl.ds(i * CH, CH)
-        v = jnp.concatenate(
-            [src[0, r].reshape(CH * ET, NF), src[1, r].reshape(CH * ET, NF)], axis=1
-        )
+        v = [(one[c, r] + two[c, r]).reshape(CH * ET, NF) for c in range(2)]
+        v = jnp.concatenate(v, axis=1)
         hi, lo = split(v)
         hl = jnp.concatenate([hi, lo], axis=0)
         n = CH * ET
@@ -251,11 +271,11 @@
                 seen = jnp.concatenate([obs[0, rows, :], obs[1, rows, :]], axis=1)
                 res[p, at] = res[p, at] - seen
 
-    def done(i, lag, earlier):
-        n = i - lag + 1
-        for at in earlier:
-            n = n + jnp.where(i >= at, 1, 0)
-        return jnp.clip(n, 0, NCH)
+    def done(i, steps):
+        n = 0
+        for at in sorted(set(steps)):
+            n = n + jnp.where(i >= at, steps.count(at), 0)
+        return n
 
     def chunk(p):
         c = p
@@ -277,12 +297,19 @@
 
         @pl.when(c < LAST * PG)
         def _():
-            @pl.when(c % PG == 0)
+            @pl.when(c == 0)
+            def _():
+                forward_half(0)
+
+            @pl.when((c > 0) & (c % PG == 0))
             def _():
                 forward(c // PG)
+
+            @pl.when((c % PG == 0) | (c == 1))
+            def _():
                 encode(c)
 
-            @pl.when(c % PG == 1)
+            @pl.when((c > 1) & (c % PG == 1))
             def _():
                 lax.fori_loop(c, c + PG - 1, lambda k, _: (encode(k), 0)[1], 0)
 
@@ -339,18 +366,19 @@
                 copy(name, c).wait_recv()
             part[y, 1 - zl, :, r] = part[y, 1 - zl, :, r] + y2l[1 - zl, :, r] + y2r[1 - zl, :, r]
             copy("z", c).start()
+            copy("g", c).start()
             res[:, r] = part[y, zl, :, r] + y2l[zl, :, r] + y2r[zl, :, r]
-            less_observed(c)
 
         @pl.when(z)
         def _():
             for name in ("l1", "r0", "l0", "r1"):
                 zcopy(name, c).wait_recv()
             res[:, r] = part[y, zl, :, r] + y2l[0, :, r] + y2r[0, :, r]
-            less_observed(c)
-            copy("h", c).start()
-            inverse(res, c, 0)
-
+            zrv[:, r] = jnp.zeros((2, CH, ET, NF), F32)
+            zgrv[:, r] = jnp.zeros((2, CH, ET, NF), F32)
+
+        less_observed(c)
+        copy("h", c).start()
         return 0
 
     def stage3(p, _):
@@ -358,18 +386,20 @@
 
         @pl.when(jnp.logical_not(early(c)))
         def _():
-            r = pl.ds(c * CH, CH)
             copy("z", c).wait_recv()
-            res[:, r] = res[:, r] + zrv[:, r]
-            copy("h", c).start()
-            inverse(res, c, 0)
-
+
+        inverse(res, zrv, c, 0)
         return 0
 
     def stage4(p, _):
         c = chunk(p)
+
+        @pl.when(jnp.logical_not(early(c)))
+        def _():
+            copy("g", c).wait_recv()
+
         copy("h", c).wait_recv()
-        inverse(zhrv, c, 1)
+        inverse(zhrv, zgrv, c, 1)
         return 0
 
     def step(i, _):
@@ -385,6 +415,8 @@
 
         @pl.when(i == ZG)
         def _():
+            forward_half(1)
+            lax.fori_loop(2, PG, lambda k, _: (encode(k), 0)[1], 0)
             forward(LAST)
             lax.fori_loop(LAST * PG, NCH, lambda k, _: (encode(k), 0)[1], 0)
 
@@ -393,18 +425,18 @@
             def _(c=c):
                 zcopy("zz", c).start()
 
-        for stage, (lag, earlier) in zip((stage1, stage2, stage3, stage4), LAGS):
-            lax.fori_loop(done(i - 1, lag, earlier), done(i, lag, earlier), stage, 0)
-        return 0
-
-    lax.fori_loop(0, NCH + LAGS[3][0] - len(LAGS[3][1]), step, 0)
+        for stage, steps in zip((stage1, stage2, stage3, stage4), STEPS):
+            lax.fori_loop(done(i - 1, steps), done(i, steps), stage, 0)
+        return 0
+
+    lax.fori_loop(0, STEPS[3][-1] + 1, step, 0)
 
     def drain(c, _):
         z = early(c)
 
         @pl.when(jnp.logical_not(z))
         def _():
-            for name in ("a1", "b1", "l1", "r0", "l0", "r1", "z"):
+            for name in ("a1", "b1", "l1", "r0", "l0", "r1", "z", "g"):
                 copy(name, c).wait_send()
 
         @pl.when(z)
@@ -423,6 +455,22 @@
         both = remote(obuf.at[xx, c], whole, xs.at[xx * 2 + c], xr.at[xx * 2 + c], device)
         both.wait_send()
         both.wait_recv()
+
+
+def turn(rows, out, held, sem):
+    def put(e):
+        return pltpu.make_async_copy(held.at[e], out.at[e], sem.at[e])
+
+    for e in range(ET):
+        def some(m, _):
+            at = pl.multiple_of(m * 128, 128)
+            held[e, pl.ds(at, 128), :] = rows[pl.ds(at * ET + e, 128, stride=ET), :]
+            return 0
+
+        lax.fori_loop(0, 16 * RL // 128, some, 0)
+        put(e).start()
+    for e in range(ET):
+        put(e).wait()
 
 
 def body(traces, phases, bins, observed):
@@ -450,6 +498,7 @@
             vmem(NY, 2, G, ET, NF),
             vmem(2, RL, ET, NF),
             vmem(2, RL, ET, NF),
+            vmem(2, RL, ET, NF),
             pltpu.VMEM((2 * NF, 1024), BF16),
             pltpu.VMEM((2 * NF, 1024), BF16),
             vmem(NX, 2, 2 * RL, ET, 128),
@@ -469,15 +518,25 @@
             dma((NCH,)),
             dma((NCH,)),
             dma((NCH,)),
+            dma((NCH,)),
+            dma((NCH,)),
             dma((8,)),
             dma((8,)),
         ],
         compiler_params=pltpu.CompilerParams(
-            collective_id=0, has_side_effects=True, vmem_limit_bytes=49 * 2**20
+            collective_id=0, has_side_effects=True, vmem_limit_bytes=51 * 2**20
         ),
         cost_estimate=pl.CostEstimate(flops=flops, bytes_accessed=22 * 2**20, transcendentals=0),
     )(*(pltpu.with_memory_space_constraint(a, pltpu.HBM) for a in arrays))
-    return rows.transpose(1, 0, 2)
+    return pl.pallas_call(
+        turn,
+        out_shape=jax.ShapeDtypeStruct((ET, 16 * RL, 128), F32),
+        in_specs=[pl.BlockSpec(memory_space=pltpu.VMEM)],
+        out_specs=pl.BlockSpec(memory_space=pl.ANY),
+        scratch_shapes=[vmem(ET, 16 * RL, 128), dma((ET,))],
+        compiler_params=pltpu.CompilerParams(vmem_limit_bytes=16 * 2**20),
+        cost_estimate=pl.CostEstimate(flops=0, bytes_accessed=8 * 2**20, transcendentals=0),
+    )(pltpu.with_memory_space_constraint(rows.reshape(16 * RL * ET, 128), pltpu.VMEM))
 
 
 def solution(mesh):

time: 99.3 us -> 91.3 us (0.919)
  Pallas kernels: 96.4 us -> 91.2 us
  local copies, waits for them, and re-layouts: 2.77 us -> 0 us
    pallas_call x1, Pallas kernels: 96.4 us -> 89 us  [body(): pl.pallas_call(kernel, out_shape=pltpu.VMEM((16 * RL, ET, 128), F32), in_...]
    transpose x1 -> x0, local copies, waits for them, and re-layouts: 2.77 us -> none  [body(): return rows.transpose(1, 0, 2)]
    pallas_call x0 -> x1, Pallas kernels: none -> 2.23 us  [body(): pl.pallas_call(turn, out_shape=jax.ShapeDtypeStruct((ET, 16 * RL, 128), F...]
where the time goes in v3:
time: 91.3 us; the launch traced here: 91.2 us
  Pallas kernels  91.2 us (100%)
    pallas_call x1, Pallas kernels, body(): pl.pallas_call(kernel, out_shape=pltpu.VMEM((16 * RL, ET, 128), F32), in_...  89 us
    pallas_call x1, Pallas kernels, body(): pl.pallas_call(turn, out_shape=jax.ShapeDtypeStruct((ET, 16 * RL, 128), F...  2.23 us

profile of v3, /device:TPU:1, one launch (start us, length us, event | category | flops | bytes accessed | tf_op | source)
XLA Modules:
  0.0 91.2 jit_solution(584899218798316273)
XLA Ops:
  0.0 89.0 %shard_map.46 = f32[1024,8,128]{2,1,0:T(8,128)S(1)} custom-call(bf16[64,64,2048]{2,1,0:T(8,128)(2,1)} %traces.1, s32[64,64]{1,0:T(8,128)} %phases.1, s32[1,256]{1,0:T(1,128)} %bitcast.5, f32[1024,256]{1,0:T(8,128)} %bitcast.4), custom_call_target="tpu_custom_call" | custom-call | flops 13958643712 | bytes 23068672 | tf_op jit(solution)/shard_map/pallas_call | solution.py:482
  89.0 2.2 %shard_map.47 = f32[8,1024,128]{2,1,0:T(8,128)} custom-call(f32[8192,128]{1,0:T(8,128)S(1)} %bitcast.3), custom_call_target="tpu_custom_call" | custom-call | bytes 8388608 | tf_op jit(solution)/shard_map/pallas_call | solution.py:531

commit v4 on v3

--- a/solution.py
+++ b/solution.py
@@ -21,17 +21,17 @@
 CH = 4
 NCH = RL // CH
 ZS = (12, 13, 14)
-SEQ = (0, 1, 2, 3, 4, 5, 6, 7, 8, 12, 9, 13, 10, 14, 11, 15)
+SEQ = (0, 1, 2, 3, 4, 5, 6, 12, 7, 8, 13, 9, 10, 14, 11, 15)
 PG = G // CH
 LAST = RL // G - 1
 STEPS = (
-    (1, 4, 4, 4, 4, 6, 7, 8, 9, 11, 12, 13, 14, 18, 18, 21),
-    (3, 4, 5, 6, 6, 8, 10, 11, 12, 13, 15, 17, 20, 21, 22, 23),
-    (5, 5, 8, 8, 9, 11, 11, 13, 13, 16, 17, 17, 21, 22, 24, 25),
-    (6, 7, 8, 10, 10, 12, 12, 13, 15, 16, 20, 20, 23, 23, 24, 26),
+    (1, 1, 4, 4, 4, 6, 7, 9, 10, 11, 11, 12, 13, 14, 19, 23),
+    (2, 4, 5, 5, 6, 8, 9, 11, 12, 12, 13, 14, 17, 21, 24, 25),
+    (4, 5, 7, 7, 10, 10, 11, 11, 12, 13, 13, 17, 21, 21, 25, 26),
+    (4, 7, 7, 10, 10, 10, 11, 12, 15, 15, 18, 21, 24, 24, 25, 26),
 )
-ZG = 1
-ZAT = (3, 7, 1)
+ZG = (1, 3)
+ZAT = (1, 3, 10)
 ET = 8
 NX = 4
 NY = 4
@@ -85,11 +85,6 @@
 
     others = [(dx, dc) for dx in (2, 1, 3, 0) for dc in (0, 1) if (dx, dc) != (0, 0)]
 
-    barrier = pltpu.get_barrier_semaphore()
-    partners = [left, right, pair, far, cross] + [owner(dx, dc)[2] for dx, dc in others]
-    for d in partners:
-        pl.semaphore_signal(barrier, inc=1, device_id=d, device_id_type=MESH)
-
     def load(g):
         return pltpu.make_async_copy(traces.at[:, pl.ds(g * G, G), :], tr.at[g], tr_sem.at[g])
 
@@ -103,6 +98,11 @@
     load_bins.start()
     load_phases.start()
     load(0).start()
+
+    barrier = pltpu.get_barrier_semaphore()
+    partners = [left, right, pair, far, cross] + [owner(dx, dc)[2] for dx, dc in others]
+    for d in partners:
+        pl.semaphore_signal(barrier, inc=1, device_id=d, device_id_type=MESH)
 
     load_phases.wait()
     cc, cs = trig(ph[...] * 32)
@@ -128,20 +128,26 @@
     cosb, sinb = trig((row * b) & (NT - 1))
     base[0] = cosb
     base[1] = sinb
-    row16 = lax.broadcasted_iota(jnp.int32, (16, NF), 0)
-    cosa, sina = trig((row16 * 128 * b[:16]) & (NT - 1))
-    base[2, 0:16] = cosa
-    base[3, 0:16] = sina
+    row8 = lax.broadcasted_iota(jnp.int32, (8, NF), 0)
+    cosa, sina = trig((row8 * 128 * b[:8]) & (NT - 1))
+    base[2, 0:8] = cosa
+    base[3, 0:8] = sina
 
     def forward_rows(a, _):
-        ca, sa = base[2, pl.ds(a, 1), :], base[3, pl.ds(a, 1), :]
+        ca, sa = base[2, pl.ds(a, 1), :], -base[3, pl.ds(a, 1), :]
         cb, sb = base[0], base[1]
         at = pl.ds(pl.multiple_of(a * 128, 128), 128)
-        ft[at, 0:NF] = (ca * cb - sa * sb).astype(BF16)
-        ft[at, NF : 2 * NF] = (-(sa * cb + ca * sb)).astype(BF16)
-        return 0
-
-    lax.fori_loop(0, 16, forward_rows, 0)
+        half = pl.ds(pl.multiple_of(a * 128 + NT // 2, 128), 128)
+        cos = ca * cb + sa * sb
+        sin = sa * cb - ca * sb
+        ft[at, 0:NF] = cos.astype(BF16)
+        ft[half, 0:NF] = (cos * flip).astype(BF16)
+        ft[at, NF : 2 * NF] = sin.astype(BF16)
+        ft[half, NF : 2 * NF] = (sin * flip).astype(BF16)
+        return 0
+
+    flip = (1 - 2 * (b[0:1] & 1)).astype(F32)
+    lax.fori_loop(0, 8, forward_rows, 0)
     load(0).wait()
     for g in (LAST, *range(1, LAST)):
         load(g).start()
@@ -201,9 +207,9 @@
         }
         return remote(*table[name])
 
-    def forward_half(h):
+    def forward(g, h):
         def tile(m, _):
-            xs_ = tr[0, pl.ds(m * 32, 32), 8 * h : 8 * h + 8].reshape(32 * 8, NT)
+            xs_ = tr[g, pl.ds(m * 32, 32), 8 * h : 8 * h + 8].reshape(32 * 8, NT)
             v = jnp.dot(xs_, ft[...], preferred_element_type=F32)
             for q in range(4):
                 for n in range(32):
@@ -213,19 +219,8 @@
 
         lax.fori_loop(0, SL // 32, tile, 0)
 
-    def forward(g):
-        load(g).wait()
-
-        def tile(m, _):
-            xs_ = tr[g, pl.ds(m * 16, 16)].reshape(16 * G, NT)
-            v = jnp.dot(xs_, ft[...], preferred_element_type=F32)
-            for q in range(4):
-                spec[q, pl.ds(pl.multiple_of(m * 16 * G, 16 * G), 16 * G), :] = v[
-                    :, q * 128 : (q + 1) * 128
-                ]
-            return 0
-
-        lax.fori_loop(0, SL // 16, tile, 0)
+    def encode_two(k):
+        lax.fori_loop(k, k + 2, lambda n, _: (encode(n), 0)[1], 0)
 
     def encode(i):
         for j in range(CH):
@@ -297,21 +292,17 @@
 
         @pl.when(c < LAST * PG)
         def _():
-            @pl.when(c == 0)
-            def _():
-                forward_half(0)
-
             @pl.when((c > 0) & (c % PG == 0))
             def _():
-                forward(c // PG)
-
-            @pl.when((c % PG == 0) | (c == 1))
+                load(c // PG).wait()
+
+            @pl.when(c % PG == 0)
+            def _():
+                forward(c // PG, 0)
+
+            @pl.when(c % PG < 2)
             def _():
                 encode(c)
-
-            @pl.when((c > 1) & (c % PG == 1))
-            def _():
-                lax.fori_loop(c, c + PG - 1, lambda k, _: (encode(k), 0)[1], 0)
 
         @pl.when(p == 0)
         def _():
@@ -329,6 +320,11 @@
             part[:, zl, :, r] = part[:, zl, :, r] + zzrv[:, :, pl.ds((c - LAST * PG) * CH, CH)]
             for name in ("a1", "b1", "l1", "r0"):
                 zcopy(name, c).start()
+
+        @pl.when((c < LAST * PG) & (c % PG == 1))
+        def _():
+            forward(c // PG, 1)
+            encode_two(c + 1)
 
     def stage1(p, _):
         c = chunk(p)
@@ -413,12 +409,16 @@
             for h in range(2):
                 load_observed(h).wait()
 
-        @pl.when(i == ZG)
-        def _():
-            forward_half(1)
-            lax.fori_loop(2, PG, lambda k, _: (encode(k), 0)[1], 0)
-            forward(LAST)
-            lax.fori_loop(LAST * PG, NCH, lambda k, _: (encode(k), 0)[1], 0)
+        @pl.when(i == ZG[0])
+        def _():
+            load(LAST).wait()
+            forward(LAST, 0)
+            encode_two(LAST * PG)
+
+        @pl.when(i == ZG[1])
+        def _():
+            forward(LAST, 1)
+            encode_two(LAST * PG + 2)
 
         for at, c in zip(ZAT, ZS):
             @pl.when(i == at)

time: 91.3 us -> 89.2 us (0.977)
  Pallas kernels: 91.2 us -> 89.1 us
    pallas_call x1, Pallas kernels: 89 us -> 86.9 us  [body(): pl.pallas_call(kernel, out_shape=pltpu.VMEM((16 * RL, ET, 128), F32), in_...]
where the time goes in v4:
time: 89.2 us; the launch traced here: 89.1 us
  Pallas kernels  89.1 us (100%)
    pallas_call x1, Pallas kernels, body(): pl.pallas_call(kernel, out_shape=pltpu.VMEM((16 * RL, ET, 128), F32), in_...  86.9 us
    pallas_call x1, Pallas kernels, body(): pl.pallas_call(turn, out_shape=jax.ShapeDtypeStruct((ET, 16 * RL, 128), F...  2.23 us

profile of v4, /device:TPU:1, one launch (start us, length us, event | category | flops | bytes accessed | tf_op | source)
XLA Modules:
  0.0 89.1 jit_solution(7831057395841489990)
XLA Ops:
  0.0 86.9 %shard_map.46 = f32[1024,8,128]{2,1,0:T(8,128)S(1)} custom-call(bf16[64,64,2048]{2,1,0:T(8,128)(2,1)} %traces.1, s32[64,64]{1,0:T(8,128)} %phases.1, s32[1,256]{1,0:T(1,128)} %bitcast.5, f32[1024,256]{1,0:T(8,128)} %bitcast.4), custom_call_target="tpu_custom_call" | custom-call | flops 13958643712 | bytes 23068672 | tf_op jit(solution)/shard_map/pallas_call | solution.py:482
  86.9 2.2 %shard_map.47 = f32[8,1024,128]{2,1,0:T(8,128)} custom-call(f32[8192,128]{1,0:T(8,128)S(1)} %bitcast.3), custom_call_target="tpu_custom_call" | custom-call | bytes 8388608 | tf_op jit(solution)/shard_map/pallas_call | solution.py:531

commit v5 on v4

--- a/solution.py
+++ b/solution.py
@@ -264,7 +264,7 @@
                 at = k * CH + j
                 rows = pl.ds(p * RL + at, ET, stride=2 * RL)
                 seen = jnp.concatenate([obs[0, rows, :], obs[1, rows, :]], axis=1)
-                res[p, at] = res[p, at] - seen
+                part[y, zl, p, at] = part[y, zl, p, at] - seen
 
     def done(i, steps):
         n = 0
@@ -329,6 +329,7 @@
     def stage1(p, _):
         c = chunk(p)
         z = early(c)
+        less_observed(c)
         r = pl.ds(c * CH, CH)
 
         @pl.when(jnp.logical_not(z))
@@ -373,7 +374,6 @@
             zrv[:, r] = jnp.zeros((2, CH, ET, NF), F32)
             zgrv[:, r] = jnp.zeros((2, CH, ET, NF), F32)
 
-        less_observed(c)
         copy("h", c).start()
         return 0
 
@@ -406,11 +406,11 @@
         @pl.when(i == 2)
         def _():
             inverse_table()
+
+        @pl.when(i == ZG[0])
+        def _():
             for h in range(2):
                 load_observed(h).wait()
-
-        @pl.when(i == ZG[0])
-        def _():
             load(LAST).wait()
             forward(LAST, 0)
             encode_two(LAST * PG)

time: 89.2 us -> 89.4 us (level)
  no operation moved by 1% of the time
where the time goes in v5:
time: 89.4 us; the launch traced here: 89.3 us
  Pallas kernels  89.3 us (100%)
    pallas_call x1, Pallas kernels, body(): pl.pallas_call(kernel, out_shape=pltpu.VMEM((16 * RL, ET, 128), F32), in_...  87 us
    pallas_call x1, Pallas kernels, body(): pl.pallas_call(turn, out_shape=jax.ShapeDtypeStruct((ET, 16 * RL, 128), F...  2.23 us

profile of v5, /device:TPU:1, one launch (start us, length us, event | category | flops | bytes accessed | tf_op | source)
XLA Modules:
  0.0 89.3 jit_solution(10294519846503845405)
XLA Ops:
  0.0 87.0 %shard_map.46 = f32[1024,8,128]{2,1,0:T(8,128)S(1)} custom-call(bf16[64,64,2048]{2,1,0:T(8,128)(2,1)} %traces.1, s32[64,64]{1,0:T(8,128)} %phases.1, s32[1,256]{1,0:T(1,128)} %bitcast.5, f32[1024,256]{1,0:T(8,128)} %bitcast.4), custom_call_target="tpu_custom_call" | custom-call | flops 13958643712 | bytes 23068672 | tf_op jit(solution)/shard_map/pallas_call | solution.py:482
  87.1 2.2 %shard_map.47 = f32[8,1024,128]{2,1,0:T(8,128)} custom-call(f32[8192,128]{1,0:T(8,128)S(1)} %bitcast.3), custom_call_target="tpu_custom_call" | custom-call | bytes 8388608 | tf_op jit(solution)/shard_map/pallas_call | solution.py:531
